TPU v7x, 256 devices: a whole 4x4x8 slice. The times are simulated.
256 devices in a mesh: dyn: 16 (over x_lo, z), phys: 16 (over x_hi, y, core).
Axes of the slice: x: 4 (x_hi: 2, x_lo: 2; x = x_hi * 2 + x_lo), y: 4, z: 8, core: 2. Of those that a mesh axis runs over, the one named last changes fastest.
Arguments:
- initial_state: float32 [72, 256, 2048], P(None, ('dyn', 'phys')), may hold values from -6 to 6
- prev_tendency: float32 [72, 256, 2048], P(None, ('dyn', 'phys')), may hold values from -3 to 3
- analysis: float32 [72, 2, 256, 256], P(None, None, ('dyn', 'phys')), may hold values from -4 to 4
- legendre: float32 [256, 16, 16, 256], P('dyn', None, 'phys'), may hold values from -6 to 6
- nudge_rate: float32 [72], replicated, may hold values from 0.1 to 2
- band_waves: int32 [256], replicated, may hold values from 0 to 255, each once
- cloudy_count: int32 [4096], P(('dyn', 'phys')), may hold values from 1 to 128, as said below
- expert_of: int32 [4096, 1], P(('dyn', 'phys')), may hold values from 0 to 15, as said below
- w_in: bfloat16 [16, 72, 1024], P('phys'), may hold values from -0.75 to 0.75
- w_mid: bfloat16 [16, 1024, 1024], P('phys'), may hold values from -0.1875 to 0.1875
- w_out: bfloat16 [16, 72, 1024], P('phys'), may hold values from -0.1875 to 0.1875
Outputs:
- final_state: float32 [72, 256, 2048], P(None, ('dyn', 'phys'))
- tendency: bfloat16 [72, 256, 2048], P(None, ('dyn', 'phys'))
Inputs may be any that keep to these rules, and one draw needn't show every extreme that they name: `band_waves`: each zonal wavenumber 0 .. 255 stands in exactly one slot. `cloudy_count`: some block of every device has 128 cloudy columns. `expert_of`: among the 16 blocks of one device no network is named more than 2 times; in every group of devices along phys one network is named exactly 2 times by each device of the group.
All inputs are finite; a program needn't handle non-finite values.
Results may differ from a plain program's by a relative error of at most 0.0065.
Values may be sent and summed in bfloat16 or wider, within the bound.
No kernel may reach another device: no remote copies, remote signals or barrier semaphores. Data moves between devices by JAX's collectives and lax.ppermute only.
A program may use at most 128 MiB of HBM per device.

v0:
```python
import math
import jax
import jax.numpy as jnp
import numpy as np
from jax import lax
from jax.sharding import PartitionSpec as P

NB_ROW = 16
CMAX = 128
TIME_STEP = 0.5
HIGH = lax.Precision.HIGH
BOTH = ("dyn", "phys")


def wave_table(waves, n_lon):
    phases = np.arange(waves)[:, None] * np.arange(n_lon)[None, :] % n_lon
    angles = phases.astype(np.float64) * (2.0 * math.pi / n_lon)
    return np.stack([np.cos(angles), -np.sin(angles)], axis=0).astype(np.float32)


def routing(expert_of, n_phys, capacity):
    experts = expert_of[:, 0]
    blocks = experts.shape[0]
    block_order = jnp.arange(blocks, dtype=jnp.int32)
    earlier = (experts[:, None] == experts[None, :]) & (block_order[None, :] < block_order[:, None])
    rank_within = jnp.sum(earlier.astype(jnp.int32), axis=1)
    target = experts * capacity + rank_within
    slots = jnp.arange(n_phys * capacity, dtype=jnp.int32)
    return (target[:, None] == slots[None, :]).astype(jnp.bfloat16)


def physics_local(initial_state, cloudy_count, expert_of, w_in, w_mid, w_out):
    levels, lat_rows, n_lon = initial_state.shape
    n_phys = lax.axis_size("phys")
    blocks = expert_of.shape[0]
    capacity = 2
    columns = initial_state.reshape(levels, blocks, n_lon // NB_ROW).astype(jnp.bfloat16)
    placing = routing(expert_of, n_phys, capacity)
    outgoing = jnp.einsum("bd,lbc->dlc", placing, columns, preferred_element_type=jnp.float32)
    outgoing = outgoing.astype(jnp.bfloat16).reshape(n_phys, capacity, levels, CMAX)
    arrived = lax.all_to_all(outgoing, "phys", split_axis=0, concat_axis=0, tiled=True)
    hidden_one = jax.nn.silu(
        jnp.einsum("qilc,lh->qihc", arrived, w_in[0], preferred_element_type=jnp.float32)
    ).astype(jnp.bfloat16)
    hidden_two = jax.nn.silu(
        jnp.einsum("qihc,hg->qigc", hidden_one, w_mid[0], preferred_element_type=jnp.float32)
    ).astype(jnp.bfloat16)
    computed = jnp.einsum(
        "qigc,lg->qilc", hidden_two, w_out[0], preferred_element_type=jnp.float32
    ).astype(jnp.bfloat16)
    returned = lax.all_to_all(computed, "phys", split_axis=0, concat_axis=0, tiled=True).reshape(
        n_phys * capacity, levels, CMAX
    )
    gathered = jnp.einsum("bd,dlc->lbc", placing, returned, preferred_element_type=jnp.float32)
    cloudy_mask = jnp.arange(CMAX, dtype=jnp.int32)[None, None, :] < cloudy_count[None, :, None]
    masked = jnp.where(cloudy_mask, gathered, 0.0).astype(jnp.bfloat16)
    return masked.reshape(levels, lat_rows, n_lon)


def on_device(
    initial_state,
    prev_tendency,
    analysis,
    legendre,
    nudge_rate,
    band_waves,
    cloudy_count,
    expert_of,
    w_in,
    w_mid,
    w_out,
):
    levels, _, n_lon = initial_state.shape
    waves = band_waves.shape[0]
    coeffs = legendre.shape[3]
    lats = waves
    table = jnp.asarray(wave_table(waves, n_lon))
    wave_ids = jnp.arange(waves, dtype=jnp.int32)
    slot_of = (band_waves[:, None] == wave_ids[None, :]).astype(jnp.bfloat16)
    me = lax.axis_index("dyn") * lax.axis_size("phys") + lax.axis_index("phys")
    own_wave = lax.dynamic_index_in_dim(band_waves, me, 0, keepdims=False)

    def to_slots(field):
        natural = jnp.einsum("lx,rmx->rml", field, table, precision=HIGH) * (1.0 / math.sqrt(n_lon))
        return jnp.einsum(
            "sm,rml->srl", slot_of, natural.astype(jnp.bfloat16), preferred_element_type=jnp.float32
        ).astype(jnp.bfloat16)

    tendency = physics_local(initial_state, cloudy_count, expert_of, w_in, w_mid, w_out)
    first = to_slots(initial_state[:, 0] + TIME_STEP * prev_tendency[:, 0])
    second = to_slots(TIME_STEP * tendency[:, 0].astype(jnp.float32))
    sent = jnp.concatenate([first, second], axis=1)
    got = lax.all_to_all(sent, BOTH, split_axis=0, concat_axis=0, tiled=True)
    got = got.reshape(lats, 2, 2, levels).astype(jnp.float32)
    own_table = (
        lax.all_to_all(
            legendre.astype(jnp.bfloat16), "phys", split_axis=0, concat_axis=2, tiled=True
        )
        .reshape(lats, coeffs)
        .astype(jnp.float32)
    )
    total_wave = (own_wave + jnp.arange(coeffs, dtype=jnp.int32)).astype(jnp.float32)
    damping = total_wave * (total_wave + 1.0) / (waves * (waves + 1.0))
    rate = nudge_rate[:, None]
    inverse = 1.0 / (1.0 + TIME_STEP * (damping[None, :] + rate))
    pulled = TIME_STEP * rate[None] * analysis[:, :, 0].transpose(1, 0, 2)

    def step(fourier):
        spectral = jnp.einsum("qrl,qk->rlk", fourier, own_table, precision=HIGH) * (
            1.0 / math.sqrt(lats)
        )
        solved = (spectral + pulled) * inverse[None]
        return jnp.einsum("rlk,qk->qrl", solved, own_table, precision=HIGH) * (
            1.0 / math.sqrt(coeffs)
        )

    again = n_lon / 2.0 / math.sqrt(waves) / math.sqrt(n_lon)
    zero_wave = own_wave == 0
    regain = jnp.stack([jnp.where(zero_wave, 2.0 * again, again), jnp.where(zero_wave, 0.0, again)])
    back = step(got[:, 0])
    back = step(regain[None, :, None] * back + got[:, 1])
    home = lax.all_to_all(back.astype(jnp.bfloat16), BOTH, split_axis=0, concat_axis=0, tiled=True)
    natural = jnp.einsum("sm,srl->rml", slot_of, home, preferred_element_type=jnp.float32)
    final = jnp.einsum("rml,rmx->lx", natural, table, precision=HIGH) * (1.0 / math.sqrt(waves))
    return (final[:, None, :], tendency)


def solution(mesh):
    in_specs = (
        P(None, ("dyn", "phys"), None),
        P(None, ("dyn", "phys"), None),
        P(None, None, ("dyn", "phys"), None),
        P("dyn", None, "phys", None),
        P(),
        P(),
        P(("dyn", "phys")),
        P(("dyn", "phys"), None),
        P("phys", None, None),
        P("phys", None, None),
        P("phys", None, None),
    )
    out_specs = (P(None, ("dyn", "phys"), None), P(None, ("dyn", "phys"), None))
    return jax.shard_map(
        on_device, mesh=mesh, in_specs=in_specs, out_specs=out_specs, check_vma=False
    )
```

profile of v0, /device:TPU:1, one launch (start us, length us, event | category | flops | bytes accessed | tf_op | source)
XLA Modules:
  0.0 137.6 jit_solution(11288121981416905189)
XLA Ops:
  0.7 1.0 convert_reduce_fusion.1
  1.7 0.7 fusion.50
  2.3 2.6 %convert_reduce_fusion = bf16[72,2048]{1,0:T(8,128)(2,1)S(1)} fusion(f32[72,1,2048]{2,1,0:T(1,128)} %param.12), kind=kLoop, calls=%fused_computation.44 | loop fusion | flops 147456 | bytes 884736 | tf_op jit(solution)/shard_map/convert_element_type | solution.py:37
  5.4 1.0 copy.45
  6.5 8.4 %all-to-all-start = ((bf16[16,2,72,128]{3,2,1,0:T(8,128)(2,1)}), bf16[16,2,72,128]{3,2,1,0:T(8,128)(2,1)S(1)}, u32[]{:S(2)}, u32[]{:S(2)}) async-start(bf16[16,2,72,128]{3,2,1,0:T(8,128)(2,1)} %copy.45), calls=%async_computation | async-start | bytes 1179648 | tf_op jit(solution)/shard_map/all_to_all | solution.py:41
  14.9 1.3 dynamic_slice.4
  16.9 2.0 %multiply_add_fusion = f32[72,1,2048]{2,1,0:T(1,128)S(1)} fusion(f32[72,1,2048]{2,1,0:T(1,128)} %param.12, f32[72,1,2048]{2,1,0:T(1,128)} %param.13), kind=kLoop, calls=%fused_computation.45 | loop fusion | flops 294912 | bytes 1769472 | tf_op jit(solution)/shard_map/add | solution.py:90
  18.9 4.3 %fusion.29 = bf16[72,2,256]{2,0,1:T(8,128)(2,1)S(1)} fusion(f32[2,256,2048]{2,1,0:T(8,128)} %constant.45.clone, f32[72,1,2048]{2,1,0:T(1,128)S(1)} %multiply_add_fusion), kind=kOutput, calls=%fused_computation.38 | convolution fusion | flops 453058560 | bytes 4857856 | tf_op jit(solution)/shard_map/lx,rmx->rml/dot_general | solution.py:84
  24.1 0.7 copy.74
  24.7 2.2 %all-to-all-done = bf16[16,2,72,128]{3,2,1,0:T(8,128)(2,1)S(1)} async-done(((bf16[16,2,72,128]{3,2,1,0:T(8,128)(2,1)}), bf16[16,2,72,128]{3,2,1,0:T(8,128)(2,1)S(1)}, u32[]{:S(2)}, u32[]{:S(2)}) %all-to-all-start) | async-done | bytes 589856 | tf_op jit(solution)/shard_map/all_to_all | solution.py:41
  26.9 6.9 %fusion.6 = bf16[16,2,1024,128]{2,3,1,0:T(8,128)(2,1)} fusion(bf16[16,2,72,128]{3,2,1,0:T(8,128)(2,1)S(1)} %all-to-all-done, bf16[1,72,1024]{2,1,0:T(8,128)(2,1)S(1)} %copy-done.9), kind=kOutput, calls=%fused_computation.10 | convolution fusion | flops 624951296 | bytes 9125888 | tf_op jit(solution)/shard_map/qilc,lh->qihc/dot_general | solution.py:43
  33.9 16.1 %fusion.17 = bf16[16,2,72,128]{3,2,1,0:T(8,128)(2,1)} fusion(bf16[16,2,1024,128]{2,3,1,0:T(8,128)(2,1)} %fusion.6, bf16[1,1024,1024]{2,1,0:T(8,128)(2,1)S(1)} %copy-done, bf16[1,72,1024]{2,1,0:T(8,128)(2,1)S(1)} %copy-done.10), kind=kOutput, calls=%fused_computation.20 | convolution fusion | flops 9215180800 | bytes 11223040 | tf_op jit(solution)/shard_map/qigc,lg->qilc/dot_general | solution.py:48
  50.0 5.2 %all-to-all-start.1 = ((bf16[16,2,72,128]{3,2,1,0:T(8,128)(2,1)}), bf16[16,2,72,128]{3,2,1,0:T(8,128)(2,1)S(1)}, u32[]{:S(2)}, u32[]{:S(2)}) async-start(bf16[16,2,72,128]{3,2,1,0:T(8,128)(2,1)} %fusion.17), calls=%async_computation.1 | async-start | bytes 1179648 | tf_op jit(solution)/shard_map/all_to_all | solution.py:51
  55.1 1.2 fusion.49
  57.6 9.5 %all-to-all-done.1 = bf16[16,2,72,128]{3,2,1,0:T(8,128)(2,1)S(1)} async-done(((bf16[16,2,72,128]{3,2,1,0:T(8,128)(2,1)}), bf16[16,2,72,128]{3,2,1,0:T(8,128)(2,1)S(1)}, u32[]{:S(2)}, u32[]{:S(2)}) %all-to-all-start.1) | async-done | bytes 589856 | tf_op jit(solution)/shard_map/all_to_all | solution.py:51
  67.1 4.5 %all-to-all-start.3 = ((bf16[16,16,1,256]{3,1,2,0:T(8,128)(2,1)}), bf16[16,16,1,256]{3,1,2,0:T(8,128)(2,1)S(1)}, u32[]{:S(2)}, u32[]{:S(2)}) async-start(bf16[16,16,1,256]{3,1,2,0:T(8,128)(2,1)} %copy.74), calls=%async_computation.3 | async-start | bytes 262144 | tf_op jit(solution)/shard_map/all_to_all | solution.py:96
  71.6 1.7 %convert_multiply_fusion = (f32[72,16,128]{2,1,0:T(8,128)S(1)}, bf16[72,16,128]{2,1,0:T(8,128)(2,1)}) fusion(s32[16]{0:T(128)} %copy-done.6, bf16[32,72,128]{2,1,0:T(8,128)(2,1)S(1)} %bitcast.167, pred[16,128]{1,0:T(8,128)(4,1)} %iota_compare_fusion.5), kind=kOutput, calls=%fused_computation.43 | convolution fusion | flops 10027520 | bytes 1476672 | tf_op jit(solution)/shard_map/bd,dlc->lbc/dot_general | solution.py:54
  73.4 4.3 %fusion.30 = bf16[72,2,256]{2,0,1:T(8,128)(2,1)S(1)} fusion(f32[72,2048,1]{1,0,2:T(8,128)S(1)} %reshape.106, f32[2,256,2048]{2,1,0:T(8,128)} %constant.45.clone), kind=kOutput, calls=%fused_computation.39 | convolution fusion | flops 453058560 | bytes 4857856 | tf_op jit(solution)/shard_map/lx,rmx->rml/dot_general | solution.py:84
  77.7 0.9 fusion.34
  78.6 0.9 pad_maximum_fusion
  79.5 0.9 copy.48
  80.4 14.5 %all-to-all-start.2 = ((bf16[256,4,72]{2,1,0:T(4,128)(2,1)}), bf16[256,4,72]{2,1,0:T(4,128)(2,1)S(1)}, u32[]{:S(2)}, u32[]{:S(2)}) async-start(bf16[256,4,72]{2,1,0:T(4,128)(2,1)} %copy.48), calls=%async_computation.2 | async-start | bytes 524288 | tf_op jit(solution)/shard_map/all_to_all | solution.py:93
  95.0 0.8 add_divide_fusion
  95.8 14.6 %all-to-all-done.2 = bf16[256,4,72]{2,1,0:T(4,128)(2,1)S(1)} async-done(((bf16[256,4,72]{2,1,0:T(4,128)(2,1)}), bf16[256,4,72]{2,1,0:T(4,128)(2,1)S(1)}, u32[]{:S(2)}, u32[]{:S(2)}) %all-to-all-start.2) | async-done | bytes 147488 | tf_op jit(solution)/shard_map/all_to_all | solution.py:93
  110.6 0.9 fusion.23
  111.7 0.9 fusion.25
  112.8 0.8 copy.53
  113.6 5.9 %all-to-all-start.4 = ((bf16[256,2,72]{2,1,0:T(2,128)(2,1)}), bf16[256,2,72]{2,1,0:T(2,128)(2,1)S(1)}, u32[]{:S(2)}, u32[]{:S(2)}) async-start(bf16[256,2,72]{2,1,0:T(2,128)(2,1)} %copy.53), calls=%async_computation.4 | async-start | bytes 262144 | tf_op jit(solution)/shard_map/all_to_all | solution.py:122
  119.5 0.8 reshape.97
  120.4 11.9 %all-to-all-done.4 = bf16[256,2,72]{2,1,0:T(2,128)(2,1)S(1)} async-done(((bf16[256,2,72]{2,1,0:T(2,128)(2,1)}), bf16[256,2,72]{2,1,0:T(2,128)(2,1)S(1)}, u32[]{:S(2)}, u32[]{:S(2)}) %all-to-all-start.4) | async-done | bytes 73760 | tf_op jit(solution)/shard_map/all_to_all | solution.py:122
  132.6 3.6 %fusion.11 = f32[72,1,2048]{2,0,1:T(8,128)S(1)} fusion(f32[2,256,72]{1,2,0:T(8,128)S(1)} %convolution_bitcast_fusion.2, f32[2,256,2048]{2,1,0:T(8,128)} %constant.45.clone), kind=kOutput, calls=%fused_computation.16 | convolution fusion | flops 453132288 | bytes 4931584 | tf_op jit(solution)/shard_map/rml,rmx->lx/dot_general | solution.py:124
  136.2 1.4 %copy.55 = f32[72,1,2048]{2,1,0:T(1,128)} copy(f32[72,1,2048]{2,0,1:T(8,128)S(1)} %fusion.11) | data formatting | bytes 1179648
  (37 shorter events, 3.8 us)
Async XLA Ops:
  0.6 33.2 %copy-start = (bf16[1,1024,1024]{2,1,0:T(8,128)(2,1)S(1)}, bf16[1,1024,1024]{2,1,0:T(8,128)(2,1)}, u32[]{:S(2)}) copy-start(bf16[1,1024,1024]{2,1,0:T(8,128)(2,1)} %param.21) | copy-start | bytes 6291460
  0.6 22.5 %copy-start.4 = (s32[256]{0:T(256)S(1)}, s32[256]{0:T(256)}, u32[]{:S(2)}) copy-start(s32[256]{0:T(256)} %param.17) | copy-start | bytes 3076
  0.7 23.4 %copy-start.3 = (f32[16,16,1,256]{3,2,1,0:T(1,128)S(1)}, f32[16,16,1,256]{3,2,1,0:T(1,128)}, u32[]{:S(2)}) copy-start(f32[16,16,1,256]{3,2,1,0:T(1,128)} %param.15) | copy-start | bytes 786436
  0.7 26.3 %copy-start.9 = (bf16[1,72,1024]{2,1,0:T(8,128)(2,1)S(1)}, bf16[1,72,1024]{2,1,0:T(8,128)(2,1)}, u32[]{:S(2)}) copy-start(bf16[1,72,1024]{2,1,0:T(8,128)(2,1)} %param.20) | copy-start | bytes 442372
  2.3 3.1 %copy-start.6 = (s32[16]{0:T(128)}, s32[16]{0:T(128)S(1)}, u32[]{:S(2)}) copy-start(s32[16]{0:T(128)S(1)} %fusion.50) | copy-start | bytes 196
  6.5 20.4 %all-to-all-start = ((bf16[16,2,72,128]{3,2,1,0:T(8,128)(2,1)}), bf16[16,2,72,128]{3,2,1,0:T(8,128)(2,1)S(1)}, u32[]{:S(2)}, u32[]{:S(2)}) async-start(bf16[16,2,72,128]{3,2,1,0:T(8,128)(2,1)} %copy.45), calls=%async_computation | async-start | bytes 1179648 | tf_op jit(solution)/shard_map/all_to_all | solution.py:41
  24.7 9.1 %copy-start.10 = (bf16[1,72,1024]{2,1,0:T(8,128)(2,1)S(1)}, bf16[1,72,1024]{2,1,0:T(8,128)(2,1)}, u32[]{:S(2)}) copy-start(bf16[1,72,1024]{2,1,0:T(8,128)(2,1)} %param.22) | copy-start | bytes 442372
  33.9 22.5 %copy-start.7 = (f32[72]{0:T(128)S(1)}, f32[72]{0:T(128)}, u32[]{:S(2)}) copy-start(f32[72]{0:T(128)} %param.16) | copy-start | bytes 868
  33.9 23.1 %copy-start.8 = (s32[16]{0:T(128)S(1)}, s32[16]{0:T(128)}, u32[]{:S(2)}) copy-start(s32[16]{0:T(128)} %param.18) | copy-start | bytes 196
  50.0 60.6 %copy-start.2 = (f32[72,2,1,256]{3,2,1,0:T(1,128)S(1)}, f32[72,2,1,256]{3,2,1,0:T(1,128)}, u32[]{:S(2)}) copy-start(f32[72,2,1,256]{3,2,1,0:T(1,128)} %param.14) | copy-start | bytes 442372
  50.0 17.2 %all-to-all-start.1 = ((bf16[16,2,72,128]{3,2,1,0:T(8,128)(2,1)}), bf16[16,2,72,128]{3,2,1,0:T(8,128)(2,1)S(1)}, u32[]{:S(2)}, u32[]{:S(2)}) async-start(bf16[16,2,72,128]{3,2,1,0:T(8,128)(2,1)} %fusion.17), calls=%async_computation.1 | async-start | bytes 1179648 | tf_op jit(solution)/shard_map/all_to_all | solution.py:51
  67.1 13.3 %all-to-all-start.3 = ((bf16[16,16,1,256]{3,1,2,0:T(8,128)(2,1)}), bf16[16,16,1,256]{3,1,2,0:T(8,128)(2,1)S(1)}, u32[]{:S(2)}, u32[]{:S(2)}) async-start(bf16[16,16,1,256]{3,1,2,0:T(8,128)(2,1)} %copy.74), calls=%async_computation.3 | async-start | bytes 262144 | tf_op jit(solution)/shard_map/all_to_all | solution.py:96
  73.4 46.2 %copy-start.1 = (bf16[72,16,128]{2,1,0:T(8,128)(2,1)S(1)}, bf16[72,16,128]{2,1,0:T(8,128)(2,1)}, u32[]{:S(2)}) copy-start(bf16[72,16,128]{2,1,0:T(8,128)(2,1)} %get-tuple-element.13) | copy-start | bytes 884740
  73.4 58.9 %copy-start.5 = (s32[256]{0:T(256)S(1)}, s32[256]{0:T(256)}, u32[]{:S(2)}) copy-start(s32[256]{0:T(256)} %param.17) | copy-start | bytes 3076
  80.4 30.0 %all-to-all-start.2 = ((bf16[256,4,72]{2,1,0:T(4,128)(2,1)}), bf16[256,4,72]{2,1,0:T(4,128)(2,1)S(1)}, u32[]{:S(2)}, u32[]{:S(2)}) async-start(bf16[256,4,72]{2,1,0:T(4,128)(2,1)} %copy.48), calls=%async_computation.2 | async-start | bytes 524288 | tf_op jit(solution)/shard_map/all_to_all | solution.py:93
  113.6 18.7 %all-to-all-start.4 = ((bf16[256,2,72]{2,1,0:T(2,128)(2,1)}), bf16[256,2,72]{2,1,0:T(2,128)(2,1)S(1)}, u32[]{:S(2)}, u32[]{:S(2)}) async-start(bf16[256,2,72]{2,1,0:T(2,128)(2,1)} %copy.53), calls=%async_computation.4 | async-start | bytes 262144 | tf_op jit(solution)/shard_map/all_to_all | solution.py:122
where the time goes:
time: 138 us
  matrix products  40.9 us (30%)
  starting transfers between devices  38.5 us (28%)
  waiting for transfers between devices  38.2 us (28%)
  other arithmetic  11.2 us (8%)
  local copies, waits for them, and re-layouts  7.28 us (5%)
  between operations  1.5 us (1%)
    dot_general x1, matrix products, physics_local(): jnp.einsum('qigc,lg->qilc', hidden_two, w_out[0], preferred_element_type=...  16.1 us
    all_to_all x1, waiting for transfers between devices, on_device(): got = lax.all_to_all(sent, BOTH, split_axis=0, concat_axis=0, tiled=True)  14.6 us
    all_to_all x1, starting transfers between devices, on_device(): got = lax.all_to_all(sent, BOTH, split_axis=0, concat_axis=0, tiled=True)  14.5 us
    all_to_all x1, waiting for transfers between devices, on_device(): lax.all_to_all(back.astype(jnp.bfloat16), BOTH, split_axis=0, concat_axis...  11.9 us
    all_to_all x1, waiting for transfers between devices, physics_local(): lax.all_to_all(computed, 'phys', split_axis=0, concat_axis=0, tiled=True)  9.52 us
    dot_general x2, matrix products, to_slots(): jnp.einsum('lx,rmx->rml', field, table, precision=HIGH)  8.53 us
    all_to_all x1, starting transfers between devices, physics_local(): lax.all_to_all(outgoing, 'phys', split_axis=0, concat_axis=0, tiled=True)  8.44 us
    dot_general x1, matrix products, physics_local(): jnp.einsum('qilc,lh->qihc', arrived, w_in[0], preferred_element_type=jnp....  6.91 us
  transfers between devices with their start and end apart: 5, of which 4 were waited for; matrix products, arithmetic and copies ran while one was open for 16% of the time, Pallas kernels for 0%

commit v1 on v0

--- a/solution.py
+++ b/solution.py
@@ -93,8 +93,14 @@
     got = lax.all_to_all(sent, BOTH, split_axis=0, concat_axis=0, tiled=True)
     got = got.reshape(lats, 2, 2, levels).astype(jnp.float32)
     own_table = (
-        lax.all_to_all(
-            legendre.astype(jnp.bfloat16), "phys", split_axis=0, concat_axis=2, tiled=True
+        jnp.concatenate(
+            lax.all_to_all(
+                jnp.stack(jnp.split(legendre.astype(jnp.bfloat16), lax.axis_size("phys"), axis=0)),
+                "phys",
+                0,
+                0,
+            ),
+            axis=2,
         )
         .reshape(lats, coeffs)
         .astype(jnp.float32)

time: 138 us -> 148 us (1.072)
  local copies, waits for them, and re-layouts: 7.28 us -> 16.4 us
  starting transfers between devices: 38.5 us -> 40.7 us
  waiting for transfers between devices: 38.2 us -> 36.2 us
    unnamed x25 -> x36, local copies, waits for them, and re-layouts: 2.18 us -> 11.4 us
    all_to_all x1, waiting for transfers between devices: 2.21 us -> 0.01 us  [physics_local(): lax.all_to_all(outgoing, 'phys', split_axis=0, concat_axis=0, tiled=True)]
    all_to_all x1, starting transfers between devices: 5.16 us -> 7.36 us  [physics_local(): lax.all_to_all(computed, 'phys', split_axis=0, concat_axis=0, tiled=True)]
  transfers between devices with their start and end apart: 5 -> 5, of which waited for: 4 -> 3; matrix products, arithmetic and copies ran while one was open for 16% -> 22% of each run, Pallas kernels for 0% -> 0%
where the time goes in v1:
time: 148 us; the launch traced here: 147 us
  matrix products  40.9 us (28%)
  starting transfers between devices  40.7 us (28%)
  waiting for transfers between devices  36.2 us (24%)
  local copies, waits for them, and re-layouts  16.4 us (11%)
  other arithmetic  11.7 us (8%)
  between operations  1.5 us (1%)
    dot_general x1, matrix products, physics_local(): jnp.einsum('qigc,lg->qilc', hidden_two, w_out[0], preferred_element_type=...  16.1 us
    all_to_all x1, waiting for transfers between devices, on_device(): got = lax.all_to_all(sent, BOTH, split_axis=0, concat_axis=0, tiled=True)  14.6 us
    all_to_all x1, starting transfers between devices, on_device(): got = lax.all_to_all(sent, BOTH, split_axis=0, concat_axis=0, tiled=True)  14.5 us
    all_to_all x1, waiting for transfers between devices, on_device(): lax.all_to_all(back.astype(jnp.bfloat16), BOTH, split_axis=0, concat_axis...  11.9 us
    unnamed x36, local copies, waits for them, and re-layouts  11.4 us
    all_to_all x1, waiting for transfers between devices, physics_local(): lax.all_to_all(computed, 'phys', split_axis=0, concat_axis=0, tiled=True)  9.61 us
    dot_general x2, matrix products, to_slots(): jnp.einsum('lx,rmx->rml', field, table, precision=HIGH)  8.53 us
    all_to_all x1, starting transfers between devices, physics_local(): lax.all_to_all(outgoing, 'phys', split_axis=0, concat_axis=0, tiled=True)  8.45 us
  transfers between devices with their start and end apart: 5, of which 3 were waited for; matrix products, arithmetic and copies ran while one was open for 22% of the time, Pallas kernels for 0%

profile of v1, /device:TPU:1, one launch (start us, length us, event | category | flops | bytes accessed | tf_op | source)
XLA Modules:
  0.0 147.4 jit_solution(851929694171021941)
XLA Ops:
  0.7 1.0 convert_reduce_fusion.1
  1.7 0.7 fusion.48
  2.3 2.6 %convert_reduce_fusion = bf16[72,2048]{1,0:T(8,128)(2,1)S(1)} fusion(f32[72,1,2048]{2,1,0:T(1,128)} %param.12), kind=kLoop, calls=%fused_computation.42 | loop fusion | flops 147456 | bytes 884736 | tf_op jit(solution)/shard_map/convert_element_type | solution.py:37
  5.4 1.0 copy.73
  6.5 8.4 %all-to-all-start.1 = ((bf16[16,2,72,128]{3,2,1,0:T(8,128)(2,1)}), bf16[16,2,72,128]{3,2,1,0:T(8,128)(2,1)S(1)}, u32[]{:S(2)}, u32[]{:S(2)}) async-start(bf16[16,2,72,128]{3,2,1,0:T(8,128)(2,1)} %copy.73), calls=%async_computation.1 | async-start | bytes 1179648 | tf_op jit(solution)/shard_map/all_to_all | solution.py:41
  14.9 1.0 copy.100
  23.0 1.3 iota_compare_fusion.5
  24.4 2.0 %multiply_add_fusion = f32[72,1,2048]{2,1,0:T(1,128)S(1)} fusion(f32[72,1,2048]{2,1,0:T(1,128)} %param.12, f32[72,1,2048]{2,1,0:T(1,128)} %param.13), kind=kLoop, calls=%fused_computation.43 | loop fusion | flops 294912 | bytes 1769472 | tf_op jit(solution)/shard_map/add | solution.py:90
  26.4 4.3 %fusion.28 = bf16[72,2,256]{2,0,1:T(8,128)(2,1)S(1)} fusion(f32[2,256,2048]{2,1,0:T(8,128)} %constant.45.clone, f32[72,1,2048]{2,1,0:T(1,128)S(1)} %multiply_add_fusion), kind=kOutput, calls=%fused_computation.37 | convolution fusion | flops 453058560 | bytes 4857856 | tf_op jit(solution)/shard_map/lx,rmx->rml/dot_general | solution.py:84
  31.5 0.6 convert_element_type.69
  34.6 6.9 %fusion.6 = bf16[16,2,1024,128]{2,3,1,0:T(8,128)(2,1)} fusion(bf16[16,2,72,128]{3,2,1,0:T(8,128)(2,1)S(1)} %all-to-all-done.1, bf16[1,72,1024]{2,1,0:T(8,128)(2,1)S(1)} %copy-done.7), kind=kOutput, calls=%fused_computation.10 | convolution fusion | flops 624951296 | bytes 9125888 | tf_op jit(solution)/shard_map/qilc,lh->qihc/dot_general | solution.py:43
  41.5 16.1 %fusion.17 = bf16[16,2,72,128]{3,2,1,0:T(8,128)(2,1)} fusion(bf16[16,2,1024,128]{2,3,1,0:T(8,128)(2,1)} %fusion.6, bf16[1,1024,1024]{2,1,0:T(8,128)(2,1)S(1)} %copy-done, bf16[1,72,1024]{2,1,0:T(8,128)(2,1)S(1)} %copy-done.8), kind=kOutput, calls=%fused_computation.20 | convolution fusion | flops 9215180800 | bytes 11223040 | tf_op jit(solution)/shard_map/qigc,lg->qilc/dot_general | solution.py:48
  57.6 7.4 %all-to-all-start.2 = ((bf16[16,2,72,128]{3,2,1,0:T(8,128)(2,1)}), bf16[16,2,72,128]{3,2,1,0:T(8,128)(2,1)S(1)}, u32[]{:S(2)}, u32[]{:S(2)}) async-start(bf16[16,2,72,128]{3,2,1,0:T(8,128)(2,1)} %fusion.17), calls=%async_computation.2 | async-start | bytes 1179648 | tf_op jit(solution)/shard_map/all_to_all | solution.py:51
  64.9 1.2 fusion.47
  67.3 9.6 %all-to-all-done.2 = bf16[16,2,72,128]{3,2,1,0:T(8,128)(2,1)S(1)} async-done(((bf16[16,2,72,128]{3,2,1,0:T(8,128)(2,1)}), bf16[16,2,72,128]{3,2,1,0:T(8,128)(2,1)S(1)}, u32[]{:S(2)}, u32[]{:S(2)}) %all-to-all-start.2) | async-done | bytes 589856 | tf_op jit(solution)/shard_map/all_to_all | solution.py:51
  76.9 4.5 %all-to-all-start = ((bf16[16,1,16,1,256]{4,2,3,1,0:T(8,128)(2,1)}), bf16[16,1,16,1,256]{4,2,3,1,0:T(8,128)(2,1)S(1)}, u32[]{:S(2)}, u32[]{:S(2)}) async-start(bf16[16,1,16,1,256]{4,2,3,1,0:T(8,128)(2,1)} %constant_dynamic-update-slice_fusion), calls=%async_computation | async-start | bytes 262144 | tf_op jit(solution)/shard_map/all_to_all | solution.py:97
  81.4 1.7 %convert_multiply_fusion = (f32[72,16,128]{2,1,0:T(8,128)S(1)}, bf16[72,16,128]{2,1,0:T(8,128)(2,1)}) fusion(s32[16]{0:T(128)} %copy-done.5, bf16[32,72,128]{2,1,0:T(8,128)(2,1)S(1)} %bitcast.222, pred[16,128]{1,0:T(8,128)(4,1)} %iota_compare_fusion.5), kind=kOutput, calls=%fused_computation.41 | convolution fusion | flops 10027520 | bytes 1476672 | tf_op jit(solution)/shard_map/bd,dlc->lbc/dot_general | solution.py:54
  83.2 4.3 %fusion.29 = bf16[72,2,256]{2,0,1:T(8,128)(2,1)S(1)} fusion(f32[72,2048,1]{1,0,2:T(8,128)S(1)} %reshape.105, f32[2,256,2048]{2,1,0:T(8,128)} %constant.45.clone), kind=kOutput, calls=%fused_computation.38 | convolution fusion | flops 453058560 | bytes 4857856 | tf_op jit(solution)/shard_map/lx,rmx->rml/dot_general | solution.py:84
  87.5 1.0 fusion.32
  88.4 0.9 pad_maximum_fusion
  89.4 0.9 copy.76
  90.2 14.5 %all-to-all-start.3 = ((bf16[256,4,72]{2,1,0:T(4,128)(2,1)}), bf16[256,4,72]{2,1,0:T(4,128)(2,1)S(1)}, u32[]{:S(2)}, u32[]{:S(2)}) async-start(bf16[256,4,72]{2,1,0:T(4,128)(2,1)} %copy.76), calls=%async_computation.3 | async-start | bytes 524288 | tf_op jit(solution)/shard_map/all_to_all | solution.py:93
  104.8 0.7 add_divide_fusion
  105.6 14.6 %all-to-all-done.3 = bf16[256,4,72]{2,1,0:T(4,128)(2,1)S(1)} async-done(((bf16[256,4,72]{2,1,0:T(4,128)(2,1)}), bf16[256,4,72]{2,1,0:T(4,128)(2,1)S(1)}, u32[]{:S(2)}, u32[]{:S(2)}) %all-to-all-start.3) | async-done | bytes 147488 | tf_op jit(solution)/shard_map/all_to_all | solution.py:93
  120.4 0.9 fusion.23
  121.5 0.9 fusion.25
  122.6 0.8 copy.79
  123.4 5.9 %all-to-all-start.4 = ((bf16[256,2,72]{2,1,0:T(2,128)(2,1)}), bf16[256,2,72]{2,1,0:T(2,128)(2,1)S(1)}, u32[]{:S(2)}, u32[]{:S(2)}) async-start(bf16[256,2,72]{2,1,0:T(2,128)(2,1)} %copy.79), calls=%async_computation.4 | async-start | bytes 262144 | tf_op jit(solution)/shard_map/all_to_all | solution.py:128
  129.3 0.8 reshape.96
  130.2 11.9 %all-to-all-done.4 = bf16[256,2,72]{2,1,0:T(2,128)(2,1)S(1)} async-done(((bf16[256,2,72]{2,1,0:T(2,128)(2,1)}), bf16[256,2,72]{2,1,0:T(2,128)(2,1)S(1)}, u32[]{:S(2)}, u32[]{:S(2)}) %all-to-all-start.4) | async-done | bytes 73760 | tf_op jit(solution)/shard_map/all_to_all | solution.py:128
  142.4 3.6 %fusion.11 = f32[72,1,2048]{2,0,1:T(8,128)S(1)} fusion(f32[2,256,72]{1,2,0:T(8,128)S(1)} %convolution_bitcast_fusion.2, f32[2,256,2048]{2,1,0:T(8,128)} %constant.45.clone), kind=kOutput, calls=%fused_computation.16 | convolution fusion | flops 453132288 | bytes 4931584 | tf_op jit(solution)/shard_map/rml,rmx->lx/dot_general | solution.py:130
  146.0 1.4 copy.81
  (49 shorter events, 12.6 us)
Async XLA Ops:
  0.6 40.9 %copy-start = (bf16[1,1024,1024]{2,1,0:T(8,128)(2,1)S(1)}, bf16[1,1024,1024]{2,1,0:T(8,128)(2,1)}, u32[]{:S(2)}) copy-start(bf16[1,1024,1024]{2,1,0:T(8,128)(2,1)} %param.21) | copy-start | bytes 6291460
  0.6 30.0 %copy-start.3 = (s32[256]{0:T(256)S(1)}, s32[256]{0:T(256)}, u32[]{:S(2)}) copy-start(s32[256]{0:T(256)} %param.17) | copy-start | bytes 3076
  0.7 30.2 %copy-start.6 = (f32[72]{0:T(128)S(1)}, f32[72]{0:T(128)}, u32[]{:S(2)}) copy-start(f32[72]{0:T(128)} %param.16) | copy-start | bytes 868
  0.7 33.9 %copy-start.7 = (bf16[1,72,1024]{2,1,0:T(8,128)(2,1)S(1)}, bf16[1,72,1024]{2,1,0:T(8,128)(2,1)}, u32[]{:S(2)}) copy-start(bf16[1,72,1024]{2,1,0:T(8,128)(2,1)} %param.20) | copy-start | bytes 442372
  2.3 3.1 %copy-start.5 = (s32[16]{0:T(128)}, s32[16]{0:T(128)S(1)}, u32[]{:S(2)}) copy-start(s32[16]{0:T(128)S(1)} %fusion.48) | copy-start | bytes 196
  6.5 28.1 %all-to-all-start.1 = ((bf16[16,2,72,128]{3,2,1,0:T(8,128)(2,1)}), bf16[16,2,72,128]{3,2,1,0:T(8,128)(2,1)S(1)}, u32[]{:S(2)}, u32[]{:S(2)}) async-start(bf16[16,2,72,128]{3,2,1,0:T(8,128)(2,1)} %copy.73), calls=%async_computation.1 | async-start | bytes 1179648 | tf_op jit(solution)/shard_map/all_to_all | solution.py:41
  34.6 6.9 %copy-start.8 = (bf16[1,72,1024]{2,1,0:T(8,128)(2,1)S(1)}, bf16[1,72,1024]{2,1,0:T(8,128)(2,1)}, u32[]{:S(2)}) copy-start(bf16[1,72,1024]{2,1,0:T(8,128)(2,1)} %param.22) | copy-start | bytes 442372
  57.6 62.8 %copy-start.2 = (f32[72,2,1,256]{3,2,1,0:T(1,128)S(1)}, f32[72,2,1,256]{3,2,1,0:T(1,128)}, u32[]{:S(2)}) copy-start(f32[72,2,1,256]{3,2,1,0:T(1,128)} %param.14) | copy-start | bytes 442372
  57.6 19.4 %all-to-all-start.2 = ((bf16[16,2,72,128]{3,2,1,0:T(8,128)(2,1)}), bf16[16,2,72,128]{3,2,1,0:T(8,128)(2,1)S(1)}, u32[]{:S(2)}, u32[]{:S(2)}) async-start(bf16[16,2,72,128]{3,2,1,0:T(8,128)(2,1)} %fusion.17), calls=%async_computation.2 | async-start | bytes 1179648 | tf_op jit(solution)/shard_map/all_to_all | solution.py:51
  76.9 13.3 %all-to-all-start = ((bf16[16,1,16,1,256]{4,2,3,1,0:T(8,128)(2,1)}), bf16[16,1,16,1,256]{4,2,3,1,0:T(8,128)(2,1)S(1)}, u32[]{:S(2)}, u32[]{:S(2)}) async-start(bf16[16,1,16,1,256]{4,2,3,1,0:T(8,128)(2,1)} %constant_dynamic-update-slice_fusion), calls=%async_computation | async-start | bytes 262144 | tf_op jit(solution)/shard_map/all_to_all | solution.py:97
  83.2 46.2 %copy-start.1 = (bf16[72,16,128]{2,1,0:T(8,128)(2,1)S(1)}, bf16[72,16,128]{2,1,0:T(8,128)(2,1)}, u32[]{:S(2)}) copy-start(bf16[72,16,128]{2,1,0:T(8,128)(2,1)} %get-tuple-element.13) | copy-start | bytes 884740
  83.2 58.9 %copy-start.4 = (s32[256]{0:T(256)S(1)}, s32[256]{0:T(256)}, u32[]{:S(2)}) copy-start(s32[256]{0:T(256)} %param.17) | copy-start | bytes 3076
  90.2 30.0 %all-to-all-start.3 = ((bf16[256,4,72]{2,1,0:T(4,128)(2,1)}), bf16[256,4,72]{2,1,0:T(4,128)(2,1)S(1)}, u32[]{:S(2)}, u32[]{:S(2)}) async-start(bf16[256,4,72]{2,1,0:T(4,128)(2,1)} %copy.76), calls=%async_computation.3 | async-start | bytes 524288 | tf_op jit(solution)/shard_map/all_to_all | solution.py:93
  123.4 18.7 %all-to-all-start.4 = ((bf16[256,2,72]{2,1,0:T(2,128)(2,1)}), bf16[256,2,72]{2,1,0:T(2,128)(2,1)S(1)}, u32[]{:S(2)}, u32[]{:S(2)}) async-start(bf16[256,2,72]{2,1,0:T(2,128)(2,1)} %copy.79), calls=%async_computation.4 | async-start | bytes 262144 | tf_op jit(solution)/shard_map/all_to_all | solution.py:128
